TPU v7x, 32 devices: a whole 2x2x4 slice. The times are simulated.
32 devices in a mesh: layer: 4 (over y, x), tok: 8 (over z, core).
Axes of the slice: x: 2, y: 2, z: 4, core: 2. Of those that a mesh axis runs over, the one named last changes fastest.
Arguments:
- inputs: bfloat16 [4, 2048, 2048], P('layer', 'tok'), may hold values from -6 to 6
- enc_weight: bfloat16 [4, 2048, 1024], P(None, 'tok'), may hold values from -0.125 to 0.125
- enc_bias: float32 [4, 1024], replicated, may hold values from -0.5 to 0.5
- dec_weight: bfloat16 [10, 1024, 2048], P(None, 'tok'), may hold values from -0.1875 to 0.1875
- dec_bias: float32 [4, 2048], replicated, may hold values from -3 to 3
Outputs:
- rebuilt: bfloat16 [4, 1, 2048, 2048], P('layer', None, 'tok')
All inputs are finite; a program needn't handle non-finite values.
Results may differ from a plain program's by a relative error of at most 0.0046.
Values may be sent and summed in bfloat16 or wider, within the bound.
A program may use at most 64 MiB of HBM per device.

v0:
```python
import jax
import jax.numpy as jnp
from jax import lax
from jax.sharding import PartitionSpec as P


def body(inputs, enc_weight, enc_bias, dec_weight, dec_bias):
    layers = enc_weight.shape[0]
    col_groups = lax.axis_size("layer") // layers
    position = lax.axis_index("layer")
    target = position // col_groups
    quarter = position % col_groups
    token_rows = inputs[0]
    tok_count = token_rows.shape[0]
    latent_count = enc_weight.shape[2]
    col_width = dec_weight.shape[2] // col_groups
    own_encoder = lax.dynamic_index_in_dim(enc_weight, target, 0, keepdims=False)
    preact = jnp.dot(
        token_rows,
        lax.all_gather(own_encoder, "tok", axis=0, tiled=True),
        preferred_element_type=jnp.float32,
    )
    own_bias = lax.dynamic_index_in_dim(enc_bias, target, 0, keepdims=False)
    latents = jnp.maximum(preact + own_bias, 0.0).astype(jnp.bfloat16)
    gathered = lax.all_gather(latents[None], "layer", axis=0, tiled=True)
    grouped = gathered.reshape(layers, col_groups * tok_count, latent_count)
    start_sum = jnp.zeros((col_groups * tok_count, col_width), jnp.float32)
    summed = start_sum
    for source in range(layers):
        usable = jnp.minimum(source, target)
        source_latents = jnp.where(
            source <= target, grouped[source], jnp.zeros_like(grouped[source])
        )
        pair_index = target * (target + 1) // 2 + usable
        weight_block = lax.dynamic_index_in_dim(dec_weight, pair_index, 0, keepdims=False)
        summed = summed + jnp.dot(
            source_latents,
            lax.all_gather(
                lax.dynamic_slice_in_dim(weight_block, quarter * col_width, col_width, 1),
                "tok",
                axis=0,
                tiled=True,
            ),
            preferred_element_type=jnp.float32,
        )
    target_bias = lax.dynamic_index_in_dim(dec_bias, target, 0, keepdims=False)
    group_bias = lax.dynamic_slice_in_dim(target_bias, quarter * col_width, col_width, 0)
    rebuilt = (summed + group_bias).astype(jnp.bfloat16)
    return rebuilt.reshape(col_groups, tok_count, col_width)[None]


def solution(mesh):
    in_specs = (P("layer", "tok", None), P(None, "tok", None), P(), P(None, "tok", None), P())
    out_specs = P("layer", None, "tok", None)
    return jax.shard_map(body, mesh=mesh, in_specs=in_specs, out_specs=out_specs, check_vma=False)
```

profile of v0, /device:TPU:0, one launch (start us, length us, event | category | flops | bytes accessed | tf_op | source)
XLA Modules:
  0.0 297.7 jit_solution(6132142810400548682)
XLA Ops:
  6.5 0.0 copy-start
  6.5 0.0 all-gather.13.cloned.1.call-start
  6.5 1.6 copy-done
  8.1 0.8 constant_dynamic-slice_fusion.6
  9.0 0.0 all-gather.13.cloned.1.call-update
  9.0 0.0 all-gather.19.cloned.1.call-start
  9.1 0.0 copy-start.1
  9.1 3.2 %constant_dynamic-slice_fusion.1 = (bf16[1,128,2048]{2,1,0:T(8,128)(2,1)}, bf16[1,128,2048]{2,1,0:T(8,128)(2,1)}, bf16[1,128,2048]{2,1,0:T(8,128)(2,1)}, bf16[1,128,2048]{2,1,0:T(8,128)(2,1)}) fusion(bf16[10,128,2048]{2,1,0:T(8,128)(2,1)} %param.8, s32[]{:T(128)S(6)} %select_n.94, s32[]{:T(128)S(6)} %select_n.86, s32[]{:T(128)S(6)} %select_n.82, s32[]{:T(128)S(6)} %select_n.90), kind=kLoop, calls=%fused_computation.34 | loop fusion | bytes 4194320 | tf_op jit(solution)/shard_map/jit(dynamic_index_in_dim)/dynamic_slice | solution.py:35
  12.3 0.0 all-gather.19.cloned.1.call-update
  12.4 0.0 all-gather.15.cloned.1.call-start
  12.4 0.7 constant_dynamic-slice_fusion.5
  13.1 45.9 %all-gather.13.cloned.1.call-done = bf16[1,2048,1024]{2,1,0:T(8,128)(2,1)} async-done(((bf16[1,256,1024]{2,1,0:T(8,128)(2,1)}), bf16[1,2048,1024]{2,1,0:T(8,128)(2,1)}) %all-gather.13.cloned.1.call-update) | async-done | bytes 4194320 | tf_op jit(solution)/shard_map/all_gather | solution.py:20
  59.0 0.0 copy-done.1
  59.0 4.3 %fusion.37 = bf16[256,1024]{0,1:T(8,128)(2,1)} fusion(bf16[1,2048,1024]{2,1,0:T(8,128)(2,1)} %all-gather.13.cloned.1.call-done, bf16[1,256,2048]{2,1,0:T(8,128)(2,1)S(1)} %copy-done.1, f32[1024]{0:T(1024)S(1)} %bitcast.45), kind=kOutput, calls=%fused_computation.19 | convolution fusion | flops 1074528256 | bytes 5771264 | tf_op jit(solution)/shard_map/dot_general | solution.py:18
  63.3 0.0 all-gather.15.cloned.1.call-update
  63.4 0.0 all-gather.17.cloned.1.call-start
  63.4 0.5 all-gather.17.cloned.1.call-update
  63.9 0.0 all-gather.21.cloned.1.call-start
  64.0 0.5 all-gather.21.cloned.1.call-update
  64.5 0.0 all-gather.23.cloned.1.call-start
  64.6 0.5 all-gather.23.cloned.1.call-update
  65.1 0.8 constant_dynamic-slice_fusion
  65.9 40.6 %all-gather.19.cloned.1.call-done = bf16[1,1024,2048]{2,1,0:T(8,128)(2,1)} async-done(((bf16[1,128,2048]{2,1,0:T(8,128)(2,1)}), bf16[1,1024,2048]{2,1,0:T(8,128)(2,1)}) %all-gather.19.cloned.1.call-update) | async-done | bytes 4194320 | tf_op jit(solution)/shard_map/all_gather | solution.py:38
  106.5 35.7 %all-gather.15.cloned.1.call-done = bf16[1024,1024]{0,1:T(8,128)(2,1)} async-done(((bf16[256,1024]{0,1:T(8,128)(2,1)}), bf16[1024,1024]{0,1:T(8,128)(2,1)}) %all-gather.15.cloned.1.call-update) | async-done | bytes 2097168 | tf_op jit(solution)/shard_map/all_gather | solution.py:25
  142.2 4.9 %fusion.4 = f32[256,2048]{1,0:T(8,128)} fusion(bf16[1,1024,2048]{2,1,0:T(8,128)(2,1)} %all-gather.19.cloned.1.call-done, bf16[1024,1024]{0,1:T(8,128)(2,1)} %all-gather.15.cloned.1.call-done, pred[]{:T(512)S(6)} %ge.13), kind=kOutput, calls=%fused_computation.4 | convolution fusion | flops 1074003968 | bytes 6815745 | tf_op jit(solution)/shard_map/dot_general | solution.py:36
  147.2 43.7 %all-gather.17.cloned.1.call-done = bf16[1,1024,2048]{2,1,0:T(8,128)(2,1)} async-done(((bf16[1,128,2048]{2,1,0:T(8,128)(2,1)}), bf16[1,1024,2048]{2,1,0:T(8,128)(2,1)}) %all-gather.17.cloned.1.call-update) | async-done | bytes 4194320 | tf_op jit(solution)/shard_map/all_gather | solution.py:38
  190.9 5.6 %fusion.10 = f32[256,2048]{1,0:T(8,128)} fusion(f32[256,2048]{1,0:T(8,128)} %fusion.4, bf16[1,1024,2048]{2,1,0:T(8,128)(2,1)} %all-gather.17.cloned.1.call-done, bf16[1024,1024]{0,1:T(8,128)(2,1)} %all-gather.15.cloned.1.call-done, pred[]{:T(512)S(6)} %ge.12), kind=kOutput, calls=%fused_computation.10 | convolution fusion | flops 1074528256 | bytes 8912897 | tf_op jit(solution)/shard_map/dot_general | solution.py:36
  196.5 41.7 %all-gather.21.cloned.1.call-done = bf16[1,1024,2048]{2,1,0:T(8,128)(2,1)} async-done(((bf16[1,128,2048]{2,1,0:T(8,128)(2,1)}), bf16[1,1024,2048]{2,1,0:T(8,128)(2,1)}) %all-gather.21.cloned.1.call-update) | async-done | bytes 4194320 | tf_op jit(solution)/shard_map/all_gather | solution.py:38
  238.2 5.6 %fusion.13 = f32[256,2048]{1,0:T(8,128)} fusion(f32[256,2048]{1,0:T(8,128)} %fusion.10, bf16[1,1024,2048]{2,1,0:T(8,128)(2,1)} %all-gather.21.cloned.1.call-done, bf16[1024,1024]{0,1:T(8,128)(2,1)} %all-gather.15.cloned.1.call-done, pred[]{:T(512)S(6)} %ge.14), kind=kOutput, calls=%fused_computation.11 | convolution fusion | flops 1074528256 | bytes 8912897 | tf_op jit(solution)/shard_map/dot_general | solution.py:36
  243.8 41.7 %all-gather.23.cloned.1.call-done = bf16[1,1024,2048]{2,1,0:T(8,128)(2,1)} async-done(((bf16[1,128,2048]{2,1,0:T(8,128)(2,1)}), bf16[1,1024,2048]{2,1,0:T(8,128)(2,1)}) %all-gather.23.cloned.1.call-update) | async-done | bytes 4194320 | tf_op jit(solution)/shard_map/all_gather | solution.py:38
  285.6 5.3 %fusion.25 = bf16[1,1,256,2048]{3,2,1,0:T(8,128)(2,1)} fusion(f32[256,2048]{1,0:T(8,128)} %fusion.13, bf16[1,1024,2048]{2,1,0:T(8,128)(2,1)} %all-gather.23.cloned.1.call-done, f32[2048]{0:T(1024)S(1)} %bitcast.44, bf16[1024,1024]{0,1:T(8,128)(2,1)} %all-gather.15.cloned.1.call-done, pred[]{:T(512)S(6)} %ge.15), kind=kOutput, calls=%fused_computation.15 | convolution fusion | flops 1075576832 | bytes 7872513 | tf_op jit(solution)/shard_map/dot_general | solution.py:36
Async XLA Ops:
  6.5 1.6 copy-start
  6.5 52.4 %all-gather.13.cloned.1.call-start = ((), (), s32[]{:S(2)}) async-start(), calls=%async_computation | async-start | bytes 4718592 | tf_op jit(solution)/shard_map/all_gather | solution.py:20
  9.0 97.5 %all-gather.19.cloned.1.call-start = ((), (), s32[]{:S(2)}) async-start(), calls=%async_computation.3 | async-start | bytes 4718592 | tf_op jit(solution)/shard_map/all_gather | solution.py:38
  9.1 49.9 %copy-start.1 = (bf16[1,256,2048]{2,1,0:T(8,128)(2,1)S(1)}, bf16[1,256,2048]{2,1,0:T(8,128)(2,1)}, u32[]{:S(2)}) copy-start(bf16[1,256,2048]{2,1,0:T(8,128)(2,1)} %param.5) | copy-start | bytes 3145732
  12.4 129.9 %all-gather.15.cloned.1.call-start = ((), (), s32[]{:S(2)}) async-start(), calls=%async_computation.1 | async-start | bytes 2621440 | tf_op jit(solution)/shard_map/all_gather | solution.py:25
  63.4 127.5 %all-gather.17.cloned.1.call-start = ((), (), s32[]{:S(2)}) async-start(), calls=%async_computation.2 | async-start | bytes 4718592 | tf_op jit(solution)/shard_map/all_gather | solution.py:38
  63.9 174.3 %all-gather.21.cloned.1.call-start = ((), (), s32[]{:S(2)}) async-start(), calls=%async_computation.4 | async-start | bytes 4718592 | tf_op jit(solution)/shard_map/all_gather | solution.py:38
  64.5 221.1 %all-gather.23.cloned.1.call-start = ((), (), s32[]{:S(2)}) async-start(), calls=%async_computation.5 | async-start | bytes 4718592 | tf_op jit(solution)/shard_map/all_gather | solution.py:38
Sparse Core Ops, SparseCore 0:
  9.1 49.8 all-gather.12
  60.6 45.8 all-gather.18
  108.3 33.8 all-gather.14
  143.7 47.1 all-gather.16
  192.3 45.8 all-gather.20
  239.7 45.8 all-gather.22
where the time goes:
time: 298 us
  waiting for transfers between devices  251 us (84%)
  matrix products  25.8 us (9%)
  between operations  13.5 us (5%)
  local copies, waits for them, and re-layouts  7.18 us (2%)
    all_gather x4, waiting for transfers between devices, body(): lax.all_gather(lax.dynamic_slice_in_dim(weight_block, quarter * col_width...  168 us
    all_gather x1, waiting for transfers between devices, body(): lax.all_gather(own_encoder, 'tok', axis=0, tiled=True)  45.9 us
    all_gather x1, waiting for transfers between devices, body(): gathered = lax.all_gather(latents[None], 'layer', axis=0, tiled=True)  35.7 us
    dot_general x4, matrix products, body(): jnp.dot(source_latents, lax.all_gather(lax.dynamic_slice_in_dim(weight_bl...  21.5 us
  transfers between devices with their start and end apart: 6, of which 6 were waited for; matrix products, arithmetic and copies ran while one was open for 8% of the time, Pallas kernels for 0%

commit v1 on v0

v1 whole, which is shorter than its diff:
```python
import jax
import jax.numpy as jnp
from jax import lax
from jax.sharding import PartitionSpec as P


def body(inputs, enc_weight, enc_bias, dec_weight, dec_bias):
    layers = enc_weight.shape[0]
    positions = lax.axis_size("layer")
    col_groups = positions // layers
    position = lax.axis_index("layer")
    own_layer = position // col_groups
    token_rows = inputs[0]
    tok_count = token_rows.shape[0]
    latent_count = enc_weight.shape[2]
    width = dec_weight.shape[2] // positions

    own_encoder = lax.dynamic_index_in_dim(enc_weight, own_layer, 0, keepdims=False)
    preact = jnp.dot(
        token_rows,
        lax.all_gather(own_encoder, "tok", axis=0, tiled=True),
        preferred_element_type=jnp.float32,
    )
    own_bias = lax.dynamic_index_in_dim(enc_bias, own_layer, 0, keepdims=False)
    latents = jnp.maximum(preact + own_bias, 0.0).astype(jnp.bfloat16)
    gathered = lax.all_gather(latents[None], "layer", axis=0, tiled=True)
    grouped = gathered.reshape(layers, col_groups * tok_count, latent_count)

    own_slice = lax.dynamic_slice_in_dim(dec_weight, position * width, width, 2)
    bias_slice = lax.dynamic_slice_in_dim(dec_bias, position * width, width, 1)
    results = []
    for target in range(layers):
        first = target * (target + 1) // 2
        weights = lax.all_gather(own_slice[first : first + target + 1], "tok", axis=1, tiled=True)
        summed = jnp.zeros((col_groups * tok_count, width), jnp.float32)
        for source in range(target + 1):
            summed = summed + jnp.dot(grouped[source], weights[source], preferred_element_type=jnp.float32)
        results.append((summed + bias_slice[target]).astype(jnp.bfloat16))
    results = jnp.stack(results)

    r = position % layers
    pieces = []
    for step in range(layers):
        block = lax.dynamic_index_in_dim(results, (r + step) % layers, 0, keepdims=False)
        perm = [
            (p, (p % layers + step) % layers * col_groups + p // layers) for p in range(positions)
        ]
        pieces.append(block if col_groups == 1 and step == 0 else lax.ppermute(block, "layer", perm))
    stacked = jnp.stack(pieces)
    order = (own_layer - jnp.arange(layers)) % layers
    placed = jnp.concatenate([stacked[order[s]] for s in range(layers)], axis=1)
    return placed.reshape(col_groups, tok_count, layers * width)[None]


def solution(mesh):
    in_specs = (P("layer", "tok", None), P(None, "tok", None), P(), P(None, "tok", None), P())
    out_specs = P("layer", None, "tok", None)
    return jax.shard_map(body, mesh=mesh, in_specs=in_specs, out_specs=out_specs, check_vma=False)
```

time: 298 us -> 262 us (0.88)
  waiting for transfers between devices: 251 us -> 199 us
  between operations: 13.5 us -> 21.4 us
  local copies, waits for them, and re-layouts: 7.18 us -> 12 us
  starting transfers between devices: 0.2 us -> 4.65 us
  matrix products: 25.8 us -> 22 us
    all_gather x4, waiting for transfers between devices: 168 us -> 113 us  [body(): lax.all_gather(own_slice[first:first + target + 1], 'tok', axis=1, tiled=...]
    slice x0 -> x6, local copies, waits for them, and re-layouts: none -> 8.52 us  [the longest x4 6.92 us: body(): own_slice[first:first + target + 1]]
    ppermute x0 -> x3, starting transfers between devices: none -> 4.44 us  [body(): lax.ppermute(block, 'layer', perm)]
    dynamic_slice x4 -> x3, local copies, waits for them, and re-layouts: 5.58 us -> 1.64 us  [the longest x1 0.83 us: body(): lax.dynamic_index_in_dim(enc_weight, own_layer, 0, keepdims=False)]
    dot_general x4 -> x10, matrix products: 21.5 us -> 17.6 us  [body(): jnp.dot(grouped[source], weights[source], preferred_element_type=jnp.floa...]
  transfers between devices with their start and end apart: 6 -> 9, of which waited for: 6 -> 7; matrix products, arithmetic and copies ran while one was open for 8% -> 11% of each run, Pallas kernels for 0% -> 0%
where the time goes in v1:
time: 262 us; the launch traced here: 261 us
  waiting for transfers between devices  199 us (76%)
  matrix products  22 us (8%)
  between operations  21.4 us (8%)
  local copies, waits for them, and re-layouts  12 us (5%)
  starting transfers between devices  4.65 us (2%)
    all_gather x4, waiting for transfers between devices, body(): lax.all_gather(own_slice[first:first + target + 1], 'tok', axis=1, tiled=...  113 us
    all_gather x1, waiting for transfers between devices, body(): lax.all_gather(own_encoder, 'tok', axis=0, tiled=True)  47.4 us
    all_gather x1, waiting for transfers between devices, body(): gathered = lax.all_gather(latents[None], 'layer', axis=0, tiled=True)  35.9 us
    dot_general x10, matrix products, body(): jnp.dot(grouped[source], weights[source], preferred_element_type=jnp.floa...  17.6 us
    slice x4, local copies, waits for them, and re-layouts, body(): own_slice[first:first + target + 1]  6.92 us
  transfers between devices with their start and end apart: 9, of which 7 were waited for; matrix products, arithmetic and copies ran while one was open for 11% of the time, Pallas kernels for 0%

profile of v1, /device:TPU:0, one launch (start us, length us, event | category | flops | bytes accessed | tf_op | source)
XLA Modules:
  0.0 261.0 jit_solution(10732694793889196601)
XLA Ops:
  6.5 1.6 copy-done
  8.1 0.8 constant_dynamic-slice_fusion.7
  9.0 1.8 constant_dynamic-slice_fusion
  10.9 0.7 constant_dynamic-slice_fusion.6
  11.6 47.4 %all-gather.17.cloned.1.call-done = bf16[1,2048,1024]{2,1,0:T(8,128)(2,1)} async-done(((bf16[1,256,1024]{2,1,0:T(8,128)(2,1)}), bf16[1,2048,1024]{2,1,0:T(8,128)(2,1)}) %all-gather.17.cloned.1.call-update) | async-done | bytes 4194320 | tf_op jit(solution)/shard_map/all_gather | solution.py:21
  59.0 4.4 %fusion.14 = bf16[256,1024]{0,1:T(8,128)(2,1)} fusion(bf16[1,2048,1024]{2,1,0:T(8,128)(2,1)} %all-gather.17.cloned.1.call-done, bf16[1,256,2048]{2,1,0:T(8,128)(2,1)S(1)} %copy-done.4, f32[1024]{0:T(1024)S(1)} %bitcast.83), kind=kOutput, calls=%fused_computation.15 | convolution fusion | flops 1074528256 | bytes 5771264 | tf_op jit(solution)/shard_map/dot_general | solution.py:19
  63.5 1.7 constant_dynamic-slice_fusion.1
  65.2 1.9 constant_dynamic-slice_fusion.5
  67.2 1.6 constant_dynamic-slice_fusion.3
  68.9 0.9 constant_dynamic-slice_fusion.2
  69.8 27.8 %all-gather.13.cloned.1.call-done = bf16[3,1024,512]{2,1,0:T(8,128)(2,1)} async-done(((bf16[3,128,512]{2,1,0:T(8,128)(2,1)}), bf16[3,1024,512]{2,1,0:T(8,128)(2,1)}) %all-gather.13.cloned.1.call-update) | async-done | bytes 3145744 | tf_op jit(solution)/shard_map/all_gather | solution.py:34
  97.6 35.9 %all-gather.19.cloned.1.call-done = bf16[1024,1024]{0,1:T(8,128)(2,1)} async-done(((bf16[256,1024]{0,1:T(8,128)(2,1)}), bf16[1024,1024]{0,1:T(8,128)(2,1)}) %all-gather.19.cloned.1.call-update) | async-done | bytes 2097168 | tf_op jit(solution)/shard_map/all_gather | solution.py:26
  133.5 2.0 fusion.26
  135.6 1.7 convolution_add_fusion.4
  137.3 1.7 fusion.22
  139.0 25.1 %all-gather.11.cloned.1.call-done = bf16[2,1024,512]{2,1,0:T(8,128)(2,1)} async-done(((bf16[2,128,512]{2,1,0:T(8,128)(2,1)}), bf16[2,1024,512]{2,1,0:T(8,128)(2,1)}) %all-gather.11.cloned.1.call-update) | async-done | bytes 2097168 | tf_op jit(solution)/shard_map/all_gather | solution.py:34
  164.1 2.0 fusion.27
  166.2 1.5 fusion.21
  167.7 44.6 %all-gather.15.cloned.1.call-done = bf16[4,1024,512]{2,1,0:T(8,128)(2,1)} async-done(((bf16[4,128,512]{2,1,0:T(8,128)(2,1)}), bf16[4,1024,512]{2,1,0:T(8,128)(2,1)}) %all-gather.15.cloned.1.call-update) | async-done | bytes 4194320 | tf_op jit(solution)/shard_map/all_gather | solution.py:34
  212.2 2.0 fusion.25
  214.2 1.9 convolution_add_fusion.2
  216.1 1.5 convolution_add_fusion.1
  217.6 1.5 fusion.23
  219.1 15.4 %all-gather.9.cloned.1.call-done = bf16[1,1024,512]{2,1,0:T(8,128)(2,1)} async-done(((bf16[1,128,512]{2,1,0:T(8,128)(2,1)}), bf16[1,1024,512]{2,1,0:T(8,128)(2,1)}) %all-gather.9.cloned.1.call-update) | async-done | bytes 1048592 | tf_op jit(solution)/shard_map/all_gather | solution.py:34
  234.6 1.8 fusion.24
  236.6 1.5 collective-permute-start
  238.1 1.5 collective-permute-start.1
  239.6 1.5 collective-permute-start.2
  241.1 0.7 fusion.41
  249.5 2.2 collective-permute-done.1
  251.8 1.2 pad_maximum_fusion.1
  253.0 1.1 maximum_bitcast_fusion
  (27 shorter events, 0.8 us)
Async XLA Ops:
  6.5 1.6 copy-start
  6.5 52.4 %copy-start.4 = (bf16[1,256,2048]{2,1,0:T(8,128)(2,1)S(1)}, bf16[1,256,2048]{2,1,0:T(8,128)(2,1)}, u32[]{:S(2)}) copy-start(bf16[1,256,2048]{2,1,0:T(8,128)(2,1)} %param.5) | copy-start | bytes 3145732
  6.5 52.4 %all-gather.17.cloned.1.call-start = ((), (), s32[]{:S(2)}) async-start(), calls=%async_computation.4 | async-start | bytes 4718592 | tf_op jit(solution)/shard_map/all_gather | solution.py:21
  9.0 88.6 %all-gather.13.cloned.1.call-start = ((), (), s32[]{:S(2)}) async-start(), calls=%async_computation.2 | async-start | bytes 3538944 | tf_op jit(solution)/shard_map/all_gather | solution.py:34
  10.8 122.7 %all-gather.19.cloned.1.call-start = ((), (), s32[]{:S(2)}) async-start(), calls=%async_computation.5 | async-start | bytes 2621440 | tf_op jit(solution)/shard_map/all_gather | solution.py:26
  63.4 100.7 %all-gather.11.cloned.1.call-start = ((), (), s32[]{:S(2)}) async-start(), calls=%async_computation.1 | async-start | bytes 2359296 | tf_op jit(solution)/shard_map/all_gather | solution.py:34
  65.1 147.1 %all-gather.15.cloned.1.call-start = ((), (), s32[]{:S(2)}) async-start(), calls=%async_computation.3 | async-start | bytes 4718592 | tf_op jit(solution)/shard_map/all_gather | solution.py:34
  67.1 167.4 %all-gather.9.cloned.1.call-start = ((), (), s32[]{:S(2)}) async-start(), calls=%async_computation | async-start | bytes 1179648 | tf_op jit(solution)/shard_map/all_gather | solution.py:34
  133.5 2.1 copy-start.2
  164.1 2.1 copy-start.3
  212.2 3.9 %copy-start.1 = (bf16[4,1024,512]{2,1,0:T(8,128)(2,1)S(1)}, bf16[4,1024,512]{2,1,0:T(8,128)(2,1)}, u32[]{:S(2)}) copy-start(bf16[4,1024,512]{2,1,0:T(8,128)(2,1)} %all-gather.15.cloned.1.call-done) | copy-start | bytes 12582916
  236.6 12.9 %collective-permute-start = (bf16[256,512]{1,0:T(8,128)(2,1)S(1)}, bf16[256,512]{1,0:T(8,128)(2,1)S(1)}, u32[]{:S(2)}, u32[]{:S(2)}) collective-permute-start(bf16[256,512]{1,0:T(8,128)(2,1)S(1)} %get-tuple-element.12), channel_id=1, source_target_pairs={{0,8},{8,16},{16,24},{24,0},{1,9},{9,17},{17,25},{25,1},{2,10},{10... | collective-permute-start | bytes 786440 | tf_op jit(solution)/shard_map/ppermute | solution.py:48
  238.1 13.6 %collective-permute-start.1 = (bf16[256,512]{1,0:T(8,128)(2,1)S(1)}, bf16[256,512]{1,0:T(8,128)(2,1)}, u32[]{:S(2)}, u32[]{:S(2)}) collective-permute-start(bf16[256,512]{1,0:T(8,128)(2,1)S(1)} %get-tuple-element.11), channel_id=1, source_target_pairs={{0,16},{8,24},{16,0},{24,8},{1,17},{9,25},{17,1},{25,9},{2,18},{10... | collective-permute-start | bytes 786440 | tf_op jit(solution)/shard_map/ppermute | solution.py:48
  239.6 12.2 %collective-permute-start.2 = (bf16[256,512]{1,0:T(8,128)(2,1)S(1)}, bf16[256,512]{1,0:T(8,128)(2,1)}, u32[]{:S(2)}, u32[]{:S(2)}) collective-permute-start(bf16[256,512]{1,0:T(8,128)(2,1)S(1)} %get-tuple-element.10), channel_id=1, source_target_pairs={{0,24},{8,0},{16,8},{24,16},{1,25},{9,1},{17,9},{25,17},{2,26},{10... | collective-permute-start | bytes 786440 | tf_op jit(solution)/shard_map/ppermute | solution.py:48
Sparse Core Ops, SparseCore 0:
  9.1 49.8 all-gather.16
  60.6 36.9 all-gather.12
  99.4 34.0 all-gather.18
  135.0 29.0 all-gather.10
  165.6 46.6 all-gather.14
  213.7 20.8 all-gather.8

commit v2 on v1

v2 whole, which is shorter than its diff:
```python
import functools

import jax
import jax.numpy as jnp
from jax import lax
from jax.experimental import pallas as pl
from jax.experimental.pallas import tpu as pltpu
from jax.sharding import PartitionSpec as P

MESH = pl.DeviceIdType.MESH


def kernel(
    positions, toks, layers,
    x_ref, enc_ref, enc_bias_ref, dec_ref, dec_bias_ref, out_ref,
    enc_buf, dec_buf, lat_buf, y_buf,
    own_sem, recv_sem, right_sem, left_sem, sibling_sem,
    lat_send, lat_recv, y_send, y_recv,
):
    groups = positions // layers
    chips = toks // 2
    me = lax.axis_index("layer")
    tok = lax.axis_index("tok")
    chip, core = tok // 2, tok % 2
    sibling = chip * 2 + 1 - core
    own_layer = me // groups
    enc_rows = enc_ref.shape[1]
    dec_rows = dec_ref.shape[1]
    width = dec_buf.shape[2]
    targets = list(range(layers))[::-1]
    chunks = layers + 1
    has_left, has_right = chip > 0, chip < chips - 1

    barrier = pltpu.get_barrier_semaphore()

    def greet(to):
        pl.semaphore_signal(barrier, inc=1, device_id=to, device_id_type=MESH)

    greet((me, sibling))
    for step in range(1, positions):
        greet((lax.rem(me + step, positions), tok))

    def part(chunk, slot):
        if chunk == 0:
            return enc_buf.at[pl.ds(pl.multiple_of(slot * enc_rows, enc_rows), enc_rows), :]
        target = targets[chunk - 1]
        first = target * (target + 1) // 2
        rows = pl.ds(pl.multiple_of(slot * dec_rows, dec_rows), dec_rows)
        return dec_buf.at[pl.ds(first, target + 1), rows, :]

    def load(chunk):
        if chunk == 0:
            source = enc_ref.at[own_layer]
        else:
            target = targets[chunk - 1]
            first = target * (target + 1) // 2
            columns = pl.ds(pl.multiple_of(me * width, width), width)
            source = dec_ref.at[pl.ds(first, target + 1), :, columns]
        return pltpu.make_async_copy(source, part(chunk, tok), own_sem.at[chunk])

    def send(chunk, slot, to, sems):
        return pltpu.make_async_remote_copy(
            src_ref=part(chunk, slot),
            dst_ref=part(chunk, slot),
            send_sem=sems.at[chunk, slot],
            recv_sem=recv_sem.at[chunk, slot],
            device_id=(me, to),
            device_id_type=MESH,
        )

    def to_right(chunk, slot):
        return send(chunk, slot, tok + 2, right_sem)

    def to_left(chunk, slot):
        return send(chunk, slot, tok - 2, left_sem)

    def to_sibling(chunk, slot):
        return send(chunk, slot, sibling, sibling_sem)

    for chunk in range(chunks):
        load(chunk).start()

    @pl.when(has_left)
    def _():
        greet((me, tok - 2))

    @pl.when(has_right)
    def _():
        greet((me, tok + 2))

    neighbours = has_left.astype(jnp.int32) + has_right.astype(jnp.int32)
    pl.semaphore_wait(barrier, positions + neighbours)

    def start_own(chunk):
        load(chunk).wait()

        @pl.when(has_right)
        def _():
            to_right(chunk, tok).start()

        @pl.when(has_left)
        def _():
            to_left(chunk, tok).start()

        to_sibling(chunk, tok).start()

    def forward(chunk):
        def step(distance, carry):
            @pl.when(chip - distance >= 0)
            def _():
                slot = tok - 2 * distance
                to_sibling(chunk, slot).wait_recv()

                @pl.when(has_right)
                def _():
                    to_right(chunk, slot).start()

                to_sibling(chunk, slot).start()

            @pl.when(chip + distance < chips)
            def _():
                slot = tok + 2 * distance
                to_sibling(chunk, slot).wait_recv()

                @pl.when(has_left)
                def _():
                    to_left(chunk, slot).start()

                to_sibling(chunk, slot).start()

            return carry

        lax.fori_loop(1, chips, step, 0)

    def wait_sibling(chunk):
        def step(index, carry):
            to_sibling(chunk, index * 2 + 1 - core).wait_recv()
            return carry

        lax.fori_loop(0, chips, step, 0)

    def drain(chunk):
        def step(index, carry):
            slot = index * 2 + core
            to_sibling(chunk, slot).wait_send()

            @pl.when(jnp.logical_and(has_right, index <= chip))
            def _():
                to_right(chunk, slot).wait_send()

            @pl.when(jnp.logical_and(has_left, index >= chip))
            def _():
                to_left(chunk, slot).wait_send()

            return carry

        lax.fori_loop(0, chips, step, 0)

    def lat_copy(step):
        return pltpu.make_async_remote_copy(
            src_ref=lat_buf.at[me],
            dst_ref=lat_buf.at[me],
            send_sem=lat_send.at[step],
            recv_sem=lat_recv.at[step],
            device_id=(lax.rem(me + step, positions), tok),
            device_id_type=MESH,
        )

    def encode():
        columns = enc_buf.shape[1]
        tile = min(256, columns)

        def step(index, carry):
            at = pl.ds(pl.multiple_of(index * tile, tile), tile)
            preact = jnp.dot(x_ref[...], enc_buf[:, at], preferred_element_type=jnp.float32)
            preact = preact + enc_bias_ref[pl.ds(own_layer, 1), at]
            lat_buf[me, :, at] = jnp.maximum(preact, 0.0).astype(lat_buf.dtype)
            return carry

        lax.fori_loop(0, columns // tile, step, 0)
        for step in range(1, positions):
            lat_copy(step).start()

    group, rank = me // layers, me % layers

    def y_dest(target):
        return target * groups + group

    def columns_of(slot):
        return pl.ds(pl.multiple_of(slot * width, width), width)

    def y_copy(target):
        return pltpu.make_async_remote_copy(
            src_ref=y_buf.at[target],
            dst_ref=out_ref.at[:, :, columns_of(rank)],
            send_sem=y_send.at[target],
            recv_sem=y_recv.at[rank],
            device_id=(y_dest(target), tok),
            device_id_type=MESH,
        )

    def y_keep(target):
        return pltpu.make_async_copy(
            y_buf.at[target], out_ref.at[:, :, columns_of(rank)], y_send.at[target]
        )

    def decode(target):
        first = target * (target + 1) // 2

        def step(index, carry):
            total = jnp.zeros((y_buf.shape[2], width), jnp.float32)
            for source in range(target + 1):
                total = total + jnp.dot(
                    lat_buf[source * groups + index],
                    dec_buf[first + source],
                    preferred_element_type=jnp.float32,
                )
            total = total + dec_bias_ref[target : target + 1, columns_of(me)]
            y_buf[target, index] = total.astype(y_buf.dtype)
            return carry

        lax.fori_loop(0, groups, step, 0)

        @pl.when(y_dest(target) == me)
        def _():
            y_keep(target).start()

        @pl.when(y_dest(target) != me)
        def _():
            y_copy(target).start()

    def compute(chunk):
        wait_sibling(chunk)
        if chunk == 0:
            encode()
            return
        if chunk == 1:
            for step in range(1, positions):
                lat_copy(step).wait_recv()
        decode(targets[chunk - 1])

    start_own(0)
    for chunk in range(chunks):
        if chunk + 1 < chunks:
            start_own(chunk + 1)
        forward(chunk)
        if chunk > 0:
            compute(chunk - 1)
    compute(chunks - 1)

    for target in range(layers):
        @pl.when(y_dest(target) == me)
        def _():
            y_keep(target).wait()

        @pl.when(y_dest(target) != me)
        def _():
            y_copy(target).wait_send()

    for slot in range(layers):
        @pl.when(lax.rem(me, groups) * layers + slot != me)
        def _():
            pltpu.make_async_remote_copy(
                src_ref=y_buf.at[0],
                dst_ref=out_ref.at[:, :, pl.ds(slot * width, width)],
                send_sem=y_send.at[0],
                recv_sem=y_recv.at[slot],
                device_id=(lax.rem(me + 1, positions), tok),
                device_id_type=MESH,
            ).wait_recv()

    for step in range(1, positions):
        lat_copy(step).wait_send()
    for chunk in range(chunks):
        drain(chunk)


def body(inputs, enc_weight, enc_bias, dec_weight, dec_bias):
    layers, enc_rows, latent_count = enc_weight.shape
    pairs, dec_rows, features = dec_weight.shape
    positions, toks = lax.axis_size("layer"), lax.axis_size("tok")
    groups = positions // layers
    tok_count = inputs.shape[1]
    width = features // positions
    chunks = layers + 1
    vmem = pl.BlockSpec(memory_space=pltpu.VMEM)
    hbm = pl.BlockSpec(memory_space=pltpu.HBM)
    dma = pltpu.SemaphoreType.DMA
    out = pl.pallas_call(
        functools.partial(kernel, positions, toks, layers),
        out_shape=jax.ShapeDtypeStruct((groups, tok_count, layers * width), jnp.bfloat16),
        in_specs=[vmem, hbm, vmem, hbm, vmem],
        out_specs=vmem,
        scratch_shapes=[
            pltpu.VMEM((enc_rows * toks, latent_count), jnp.bfloat16),
            pltpu.VMEM((pairs, dec_rows * toks, width), jnp.bfloat16),
            pltpu.VMEM((positions, tok_count, latent_count), jnp.bfloat16),
            pltpu.VMEM((layers, groups, tok_count, width), jnp.bfloat16),
            dma((chunks,)),
            dma((chunks, toks)),
            dma((chunks, toks)),
            dma((chunks, toks)),
            dma((chunks, toks)),
            dma((positions,)),
            dma((positions,)),
            dma((layers,)),
            dma((layers,)),
        ],
        compiler_params=pltpu.CompilerParams(
            collective_id=0, has_side_effects=True, vmem_limit_bytes=48 * 1024 * 1024
        ),
        cost_estimate=pl.CostEstimate(
            flops=2 * tok_count * latent_count * features * (1 + pairs // layers),
            bytes_accessed=8 * 1024 * 1024,
            transcendentals=0,
        ),
    )(inputs[0], enc_weight, enc_bias, dec_weight, dec_bias)
    return out[None]


def solution(mesh):
    in_specs = (P("layer", "tok", None), P(None, "tok", None), P(), P(None, "tok", None), P())
    out_specs = P("layer", None, "tok", None)
    return jax.shard_map(body, mesh=mesh, in_specs=in_specs, out_specs=out_specs, check_vma=False)
```

time: 262 us -> 147 us (0.56)
  waiting for transfers between devices: 199 us -> 0 us
  Pallas kernels: 0 us -> 142 us
  matrix products: 22 us -> 0 us
  between operations: 21.4 us -> 0.01 us
  local copies, waits for them, and re-layouts: 12 us -> 5.26 us
  starting transfers between devices: 4.65 us -> 0 us
    all_gather x6 -> x0, waiting for transfers between devices: 196 us -> none  [the longest x4 113 us: body(): lax.all_gather(own_slice[first:first + target + 1], 'tok', axis=1, tiled=...]
    pallas_call x0 -> x1, Pallas kernels: none -> 142 us  [body(): pl.pallas_call(functools.partial(kernel, positions, toks, layers), out_sh...]
    dot_general x11 -> x0, matrix products: 22 us -> none  [the longest x10 17.6 us: body(): jnp.dot(grouped[source], weights[source], preferred_element_type=jnp.floa...]
    slice x6 -> x0, local copies, waits for them, and re-layouts: 8.52 us -> none  [the longest x4 6.92 us: body(): own_slice[first:first + target + 1]]
    ppermute x3 -> x0, starting transfers between devices: 4.44 us -> none  [body(): lax.ppermute(block, 'layer', perm)]
    unnamed x10 -> x9, local copies, waits for them, and re-layouts: 1.74 us -> 5.26 us
  transfers between devices with their start and end apart: 9 -> 0, of which waited for: 7 -> 0; matrix products, arithmetic and copies ran while one was open for 11% -> 0% of each run, Pallas kernels for 0% -> 0%
where the time goes in v2:
time: 147 us
  Pallas kernels  142 us (97%)
  local copies, waits for them, and re-layouts  5.26 us (4%)
    pallas_call x1, Pallas kernels, body(): pl.pallas_call(functools.partial(kernel, positions, toks, layers), out_sh...  142 us
    unnamed x9, local copies, waits for them, and re-layouts  5.26 us

profile of v2, /device:TPU:0, one launch (start us, length us, event | category | flops | bytes accessed | tf_op | source)
XLA Modules:
  0.0 147.0 jit_solution(14821349780112637937)
XLA Ops:
  0.0 0.0 copy-start
  0.0 1.6 %copy-done = bf16[4,256,1024]{2,1,0:T(8,128)(2,1)S(1)} copy-done((bf16[4,256,1024]{2,1,0:T(8,128)(2,1)S(1)}, bf16[4,256,1024]{2,1,0:T(8,128)(2,1)}, u32[]{:S(2)}) %copy-start) | copy-done | bytes 2097176
  1.6 0.0 copy-start.1
  1.6 1.2 copy-done.1
  2.8 0.0 copy-start.2
  2.8 0.8 copy-done.2
  3.6 0.0 copy-start.3
  3.6 0.7 copy-done.3
  4.3 141.7 %shard_map.55 = bf16[1,256,2048]{2,1,0:T(8,128)(2,1)S(1)} custom-call(bf16[256,2048]{1,0:T(8,128)(2,1)S(1)} %bitcast.3, bf16[4,256,1024]{2,1,0:T(8,128)(2,1)S(1)} %copy-done, f32[4,1024]{1,0:T(4,128)S(1)} %copy-done.3, bf16[10,128,2048]{2,1,0:T(8,128)(2,1)} %dec_ref.1, f32[4,2048]{1,0:T(4,128)S(1)} %copy-done.2), custom_call_target="tpu_custom_call" | custom-call | flops 3221225472 | bytes 8388608 | tf_op jit(solution)/shard_map/pallas_call | solution.py:289
  146.0 1.0 copy.7
Async XLA Ops:
  0.0 1.6 %copy-start = (bf16[4,256,1024]{2,1,0:T(8,128)(2,1)S(1)}, bf16[4,256,1024]{2,1,0:T(8,128)(2,1)}, u32[]{:S(2)}) copy-start(bf16[4,256,1024]{2,1,0:T(8,128)(2,1)} %enc_ref.1) | copy-start | bytes 6291460
  1.6 1.2 copy-start.1
  2.8 0.8 copy-start.2
  3.6 0.7 copy-start.3

commit v3 on v2

--- a/solution.py
+++ b/solution.py
@@ -13,9 +13,9 @@
 def kernel(
     positions, toks, layers,
     x_ref, enc_ref, enc_bias_ref, dec_ref, dec_bias_ref, out_ref,
-    enc_buf, dec_buf, lat_buf, y_buf,
+    x_buf, enc_buf, dec_buf, lat_buf, y_buf,
     own_sem, recv_sem, right_sem, left_sem, sibling_sem,
-    lat_send, lat_recv, y_send, y_recv,
+    x_send, x_recv, lat_send, lat_recv, y_send, y_recv,
 ):
     groups = positions // layers
     chips = toks // 2
@@ -31,6 +31,16 @@
     chunks = layers + 1
     has_left, has_right = chip > 0, chip < chips - 1
 
+    folded = chips >= 4
+    lowest, highest = (1, chips - 2) if folded else (0, chips - 1)
+    is_worker = jnp.logical_and(chip >= lowest, chip <= highest)
+    is_end = jnp.logical_not(is_worker)
+    paired = jnp.logical_or(chip <= 1, chip >= chips - 2) if folded else chip < 0
+    is_helper = jnp.logical_and(paired, is_worker)
+    outwards = jnp.logical_or(chip == 0, chip == chips - 2)
+    partner = tok + jnp.where(outwards, 2, -2)
+    can_left, can_right = chip > lowest, chip < highest
+
     barrier = pltpu.get_barrier_semaphore()
 
     def greet(to):
@@ -77,9 +87,27 @@
     def to_sibling(chunk, slot):
         return send(chunk, slot, sibling, sibling_sem)
 
+    def to_partner(chunk):
+        return send(chunk, tok, partner, right_sem)
+
+    def x_copy():
+        return pltpu.make_async_remote_copy(
+            src_ref=x_ref,
+            dst_ref=x_buf,
+            send_sem=x_send.at[0],
+            recv_sem=x_recv.at[0],
+            device_id=(me, partner),
+            device_id_type=MESH,
+        )
+
     for chunk in range(chunks):
         load(chunk).start()
 
+    @pl.when(paired)
+    def _():
+        for step in range(1, positions):
+            greet((lax.rem(me + step, positions), partner))
+
     @pl.when(has_left)
     def _():
         greet((me, tok - 2))
@@ -89,16 +117,17 @@
         greet((me, tok + 2))
 
     neighbours = has_left.astype(jnp.int32) + has_right.astype(jnp.int32)
-    pl.semaphore_wait(barrier, positions + neighbours)
+    crossing = paired.astype(jnp.int32) * (positions - 1)
+    pl.semaphore_wait(barrier, positions + neighbours + crossing)
 
     def start_own(chunk):
         load(chunk).wait()
 
-        @pl.when(has_right)
+        @pl.when(can_right)
         def _():
             to_right(chunk, tok).start()
 
-        @pl.when(has_left)
+        @pl.when(can_left)
         def _():
             to_left(chunk, tok).start()
 
@@ -111,7 +140,7 @@
                 slot = tok - 2 * distance
                 to_sibling(chunk, slot).wait_recv()
 
-                @pl.when(has_right)
+                @pl.when(can_right)
                 def _():
                     to_right(chunk, slot).start()
 
@@ -122,7 +151,7 @@
                 slot = tok + 2 * distance
                 to_sibling(chunk, slot).wait_recv()
 
-                @pl.when(has_left)
+                @pl.when(can_left)
                 def _():
                     to_left(chunk, slot).start()
 
@@ -144,11 +173,11 @@
             slot = index * 2 + core
             to_sibling(chunk, slot).wait_send()
 
-            @pl.when(jnp.logical_and(has_right, index <= chip))
+            @pl.when(jnp.logical_and(can_right, index <= chip))
             def _():
                 to_right(chunk, slot).wait_send()
 
-            @pl.when(jnp.logical_and(has_left, index >= chip))
+            @pl.when(jnp.logical_and(can_left, index >= chip))
             def _():
                 to_left(chunk, slot).wait_send()
 
@@ -156,30 +185,31 @@
 
         lax.fori_loop(0, chips, step, 0)
 
-    def lat_copy(step):
+    def lat_copy(part_of, step):
         return pltpu.make_async_remote_copy(
-            src_ref=lat_buf.at[me],
-            dst_ref=lat_buf.at[me],
-            send_sem=lat_send.at[step],
-            recv_sem=lat_recv.at[step],
+            src_ref=lat_buf.at[part_of, me],
+            dst_ref=lat_buf.at[part_of, me],
+            send_sem=lat_send.at[part_of, step],
+            recv_sem=lat_recv.at[part_of, step],
             device_id=(lax.rem(me + step, positions), tok),
             device_id_type=MESH,
         )
 
-    def encode():
+    def encode(part_of):
         columns = enc_buf.shape[1]
         tile = min(256, columns)
+        tokens = x_buf if part_of else x_ref
 
         def step(index, carry):
             at = pl.ds(pl.multiple_of(index * tile, tile), tile)
-            preact = jnp.dot(x_ref[...], enc_buf[:, at], preferred_element_type=jnp.float32)
+            preact = jnp.dot(tokens[...], enc_buf[:, at], preferred_element_type=jnp.float32)
             preact = preact + enc_bias_ref[pl.ds(own_layer, 1), at]
-            lat_buf[me, :, at] = jnp.maximum(preact, 0.0).astype(lat_buf.dtype)
+            lat_buf[part_of, me, :, at] = jnp.maximum(preact, 0.0).astype(lat_buf.dtype)
             return carry
 
         lax.fori_loop(0, columns // tile, step, 0)
         for step in range(1, positions):
-            lat_copy(step).start()
+            lat_copy(part_of, step).start()
 
     group, rank = me // layers, me % layers
 
@@ -189,90 +219,130 @@
     def columns_of(slot):
         return pl.ds(pl.multiple_of(slot * width, width), width)
 
-    def y_copy(target):
+    def y_copy(part_of, target):
         return pltpu.make_async_remote_copy(
-            src_ref=y_buf.at[target],
+            src_ref=y_buf.at[part_of, target],
             dst_ref=out_ref.at[:, :, columns_of(rank)],
-            send_sem=y_send.at[target],
+            send_sem=y_send.at[part_of, target],
             recv_sem=y_recv.at[rank],
-            device_id=(y_dest(target), tok),
+            device_id=(y_dest(target), partner if part_of else tok),
             device_id_type=MESH,
         )
 
     def y_keep(target):
         return pltpu.make_async_copy(
-            y_buf.at[target], out_ref.at[:, :, columns_of(rank)], y_send.at[target]
-        )
-
-    def decode(target):
+            y_buf.at[0, target], out_ref.at[:, :, columns_of(rank)], y_send.at[0, target]
+        )
+
+    def decode(part_of, target):
         first = target * (target + 1) // 2
 
         def step(index, carry):
-            total = jnp.zeros((y_buf.shape[2], width), jnp.float32)
+            total = jnp.zeros((y_buf.shape[3], width), jnp.float32)
             for source in range(target + 1):
                 total = total + jnp.dot(
-                    lat_buf[source * groups + index],
+                    lat_buf[part_of, source * groups + index],
                     dec_buf[first + source],
                     preferred_element_type=jnp.float32,
                 )
             total = total + dec_bias_ref[target : target + 1, columns_of(me)]
-            y_buf[target, index] = total.astype(y_buf.dtype)
+            y_buf[part_of, target, index] = total.astype(y_buf.dtype)
             return carry
 
         lax.fori_loop(0, groups, step, 0)
 
+        if part_of:
+            y_copy(part_of, target).start()
+            return
+
         @pl.when(y_dest(target) == me)
         def _():
             y_keep(target).start()
 
         @pl.when(y_dest(target) != me)
         def _():
-            y_copy(target).start()
-
-    def compute(chunk):
-        wait_sibling(chunk)
+            y_copy(part_of, target).start()
+
+    def compute(chunk, part_of):
         if chunk == 0:
-            encode()
+            if part_of:
+                x_copy().wait_recv()
+            encode(part_of)
             return
         if chunk == 1:
             for step in range(1, positions):
-                lat_copy(step).wait_recv()
-        decode(targets[chunk - 1])
-
-    start_own(0)
-    for chunk in range(chunks):
-        if chunk + 1 < chunks:
-            start_own(chunk + 1)
-        forward(chunk)
-        if chunk > 0:
-            compute(chunk - 1)
-    compute(chunks - 1)
-
-    for target in range(layers):
-        @pl.when(y_dest(target) == me)
-        def _():
-            y_keep(target).wait()
-
-        @pl.when(y_dest(target) != me)
-        def _():
-            y_copy(target).wait_send()
+                lat_copy(part_of, step).wait_recv()
+        decode(part_of, targets[chunk - 1])
+
+    def compute_both(chunk):
+        wait_sibling(chunk)
+        compute(chunk, 0)
+
+        @pl.when(is_helper)
+        def _():
+            compute(chunk, 1)
+
+    @pl.when(is_end)
+    def _():
+        sends = [to_partner(0), x_copy()] + [to_partner(chunk) for chunk in range(1, chunks)]
+        loads = [load(0), None] + [load(chunk) for chunk in range(1, chunks)]
+        for index in range(chunks + 1):
+            if index >= 2:
+                sends[index - 2].wait_send()
+            if loads[index] is not None:
+                loads[index].wait()
+            sends[index].start()
+        sends[chunks - 1].wait_send()
+        sends[chunks].wait_send()
+
+    @pl.when(is_worker)
+    def _():
+        start_own(0)
+        begun = 1
+        for chunk in range(chunks):
+            ahead = min(chunks, chunk + (2 if chunk == 0 else 3))
+            for later in range(begun, ahead):
+                start_own(later)
+            begun = max(begun, ahead)
+            forward(chunk)
+            if chunk > 0:
+                compute_both(chunk - 1)
+        compute_both(chunks - 1)
+
+        for target in range(layers):
+            @pl.when(y_dest(target) == me)
+            def _():
+                y_keep(target).wait()
+
+            @pl.when(y_dest(target) != me)
+            def _():
+                y_copy(0, target).wait_send()
 
     for slot in range(layers):
-        @pl.when(lax.rem(me, groups) * layers + slot != me)
+        @pl.when(jnp.logical_or(is_end, lax.rem(me, groups) * layers + slot != me))
         def _():
             pltpu.make_async_remote_copy(
-                src_ref=y_buf.at[0],
+                src_ref=y_buf.at[0, 0],
                 dst_ref=out_ref.at[:, :, pl.ds(slot * width, width)],
-                send_sem=y_send.at[0],
+                send_sem=y_send.at[0, 0],
                 recv_sem=y_recv.at[slot],
                 device_id=(lax.rem(me + 1, positions), tok),
                 device_id_type=MESH,
             ).wait_recv()
 
-    for step in range(1, positions):
-        lat_copy(step).wait_send()
-    for chunk in range(chunks):
-        drain(chunk)
+    @pl.when(is_worker)
+    def _():
+        for step in range(1, positions):
+            lat_copy(0, step).wait_send()
+        for chunk in range(chunks):
+            drain(chunk)
+
+    @pl.when(is_helper)
+    def _():
+        for step in range(1, positions):
+            lat_copy(1, step).wait_send()
+        for target in range(layers):
+            y_copy(1, target).wait_send()
 
 
 def body(inputs, enc_weight, enc_bias, dec_weight, dec_bias):
@@ -292,22 +362,25 @@
         in_specs=[vmem, hbm, vmem, hbm, vmem],
         out_specs=vmem,
         scratch_shapes=[
+            pltpu.VMEM((tok_count, enc_rows * toks), jnp.bfloat16),
             pltpu.VMEM((enc_rows * toks, latent_count), jnp.bfloat16),
             pltpu.VMEM((pairs, dec_rows * toks, width), jnp.bfloat16),
-            pltpu.VMEM((positions, tok_count, latent_count), jnp.bfloat16),
-            pltpu.VMEM((layers, groups, tok_count, width), jnp.bfloat16),
+            pltpu.VMEM((2, positions, tok_count, latent_count), jnp.bfloat16),
+            pltpu.VMEM((2, layers, groups, tok_count, width), jnp.bfloat16),
             dma((chunks,)),
             dma((chunks, toks)),
             dma((chunks, toks)),
             dma((chunks, toks)),
             dma((chunks, toks)),
-            dma((positions,)),
-            dma((positions,)),
-            dma((layers,)),
+            dma((1,)),
+            dma((1,)),
+            dma((2, positions)),
+            dma((2, positions)),
+            dma((2, layers)),
             dma((layers,)),
         ],
         compiler_params=pltpu.CompilerParams(
-            collective_id=0, has_side_effects=True, vmem_limit_bytes=48 * 1024 * 1024
+            collective_id=0, has_side_effects=True, vmem_limit_bytes=58 * 1024 * 1024
         ),
         cost_estimate=pl.CostEstimate(
             flops=2 * tok_count * latent_count * features * (1 + pairs // layers),

time: 147 us -> 155 us (1.054)
  Pallas kernels: 142 us -> 153 us
  local copies, waits for them, and re-layouts: 5.26 us -> 2.3 us
    pallas_call x1, Pallas kernels: 142 us -> 153 us  [body(): pl.pallas_call(functools.partial(kernel, positions, toks, layers), out_sh...]
    unnamed x9 -> x1, local copies, waits for them, and re-layouts: 5.26 us -> 2.3 us
where the time goes in v3:
time: 155 us
  Pallas kernels  153 us (99%)
  local copies, waits for them, and re-layouts  2.3 us (1%)
    pallas_call x1, Pallas kernels, body(): pl.pallas_call(functools.partial(kernel, positions, toks, layers), out_sh...  153 us

profile of v3, /device:TPU:0, one launch (start us, length us, event | category | flops | bytes accessed | tf_op | source)
XLA Modules:
  0.0 155.0 jit_solution(14061408952330734516)
XLA Ops:
  0.0 152.7 %shard_map.55 = bf16[1,256,2048]{2,1,0:T(8,128)(2,1)} custom-call(bf16[256,2048]{1,0:T(8,128)(2,1)} %bitcast.3, bf16[4,256,1024]{2,1,0:T(8,128)(2,1)} %enc_ref.1, f32[4,1024]{1,0:T(4,128)} %enc_bias_ref.1, bf16[10,128,2048]{2,1,0:T(8,128)(2,1)} %dec_ref.1, f32[4,2048]{1,0:T(4,128)} %dec_bias_ref.1), custom_call_target="tpu_custom_call" | custom-call | flops 3221225472 | bytes 8388608 | tf_op jit(solution)/shard_map/pallas_call | solution.py:359
  152.7 2.3 %copy.7 = bf16[1,1,256,2048]{3,2,1,0:T(8,128)(2,1)} copy(bf16[1,1,256,2048]{3,2,1,0:T(8,128)(2,1)} %bitcast.2) | data formatting | bytes 2097152

commit v4 on v3

--- a/solution.py
+++ b/solution.py
@@ -26,9 +26,9 @@
     own_layer = me // groups
     enc_rows = enc_ref.shape[1]
     dec_rows = dec_ref.shape[1]
-    width = dec_buf.shape[2]
-    targets = list(range(layers))[::-1]
-    chunks = layers + 1
+    subs, _, _, sub = dec_buf.shape
+    width = subs * sub
+    chunks = subs + 1
     has_left, has_right = chip > 0, chip < chips - 1
 
     folded = chips >= 4
@@ -53,19 +53,15 @@
     def part(chunk, slot):
         if chunk == 0:
             return enc_buf.at[pl.ds(pl.multiple_of(slot * enc_rows, enc_rows), enc_rows), :]
-        target = targets[chunk - 1]
-        first = target * (target + 1) // 2
         rows = pl.ds(pl.multiple_of(slot * dec_rows, dec_rows), dec_rows)
-        return dec_buf.at[pl.ds(first, target + 1), rows, :]
+        return dec_buf.at[chunk - 1, :, rows, :]
 
     def load(chunk):
         if chunk == 0:
             source = enc_ref.at[own_layer]
         else:
-            target = targets[chunk - 1]
-            first = target * (target + 1) // 2
-            columns = pl.ds(pl.multiple_of(me * width, width), width)
-            source = dec_ref.at[pl.ds(first, target + 1), :, columns]
+            columns = pl.ds(pl.multiple_of(me * width + (chunk - 1) * sub, sub), sub)
+            source = dec_ref.at[:, :, columns]
         return pltpu.make_async_copy(source, part(chunk, tok), own_sem.at[chunk])
 
     def send(chunk, slot, to, sems):
@@ -216,52 +212,54 @@
     def y_dest(target):
         return target * groups + group
 
-    def columns_of(slot):
-        return pl.ds(pl.multiple_of(slot * width, width), width)
-
-    def y_copy(part_of, target):
+    def columns_of(slot, index):
+        return pl.ds(pl.multiple_of(slot * width + index * sub, sub), sub)
+
+    def y_copy(part_of, target, index):
         return pltpu.make_async_remote_copy(
-            src_ref=y_buf.at[part_of, target],
-            dst_ref=out_ref.at[:, :, columns_of(rank)],
-            send_sem=y_send.at[part_of, target],
-            recv_sem=y_recv.at[rank],
+            src_ref=y_buf.at[part_of, target, index],
+            dst_ref=out_ref.at[:, :, columns_of(rank, index)],
+            send_sem=y_send.at[part_of, target, index],
+            recv_sem=y_recv.at[rank, index],
             device_id=(y_dest(target), partner if part_of else tok),
             device_id_type=MESH,
         )
 
-    def y_keep(target):
+    def y_keep(target, index):
         return pltpu.make_async_copy(
-            y_buf.at[0, target], out_ref.at[:, :, columns_of(rank)], y_send.at[0, target]
+            y_buf.at[0, target, index],
+            out_ref.at[:, :, columns_of(rank, index)],
+            y_send.at[0, target, index],
         )
 
-    def decode(part_of, target):
+    def decode(part_of, target, at):
         first = target * (target + 1) // 2
 
         def step(index, carry):
-            total = jnp.zeros((y_buf.shape[3], width), jnp.float32)
+            total = jnp.zeros((y_buf.shape[4], sub), jnp.float32)
             for source in range(target + 1):
                 total = total + jnp.dot(
                     lat_buf[part_of, source * groups + index],
-                    dec_buf[first + source],
+                    dec_buf[at, first + source],
                     preferred_element_type=jnp.float32,
                 )
-            total = total + dec_bias_ref[target : target + 1, columns_of(me)]
-            y_buf[part_of, target, index] = total.astype(y_buf.dtype)
+            total = total + dec_bias_ref[target : target + 1, columns_of(me, at)]
+            y_buf[part_of, target, at, index] = total.astype(y_buf.dtype)
             return carry
 
         lax.fori_loop(0, groups, step, 0)
 
         if part_of:
-            y_copy(part_of, target).start()
+            y_copy(part_of, target, at).start()
             return
 
         @pl.when(y_dest(target) == me)
         def _():
-            y_keep(target).start()
+            y_keep(target, at).start()
 
         @pl.when(y_dest(target) != me)
         def _():
-            y_copy(part_of, target).start()
+            y_copy(part_of, target, at).start()
 
     def compute(chunk, part_of):
         if chunk == 0:
@@ -272,7 +270,8 @@
         if chunk == 1:
             for step in range(1, positions):
                 lat_copy(part_of, step).wait_recv()
-        decode(part_of, targets[chunk - 1])
+        for target in range(layers):
+            decode(part_of, target, chunk - 1)
 
     def compute_both(chunk):
         wait_sibling(chunk)
@@ -305,30 +304,33 @@
                 start_own(later)
             begun = max(begun, ahead)
             forward(chunk)
-            if chunk > 0:
-                compute_both(chunk - 1)
-        compute_both(chunks - 1)
+            if chunk == 1:
+                compute_both(0)
+        for chunk in range(0 if chunks <= 1 else 1, chunks):
+            compute_both(chunk)
 
         for target in range(layers):
-            @pl.when(y_dest(target) == me)
-            def _():
-                y_keep(target).wait()
-
-            @pl.when(y_dest(target) != me)
-            def _():
-                y_copy(0, target).wait_send()
+            for index in range(subs):
+                @pl.when(y_dest(target) == me)
+                def _():
+                    y_keep(target, index).wait()
+
+                @pl.when(y_dest(target) != me)
+                def _():
+                    y_copy(0, target, index).wait_send()
 
     for slot in range(layers):
         @pl.when(jnp.logical_or(is_end, lax.rem(me, groups) * layers + slot != me))
         def _():
-            pltpu.make_async_remote_copy(
-                src_ref=y_buf.at[0, 0],
-                dst_ref=out_ref.at[:, :, pl.ds(slot * width, width)],
-                send_sem=y_send.at[0, 0],
-                recv_sem=y_recv.at[slot],
-                device_id=(lax.rem(me + 1, positions), tok),
-                device_id_type=MESH,
-            ).wait_recv()
+            for index in range(subs):
+                pltpu.make_async_remote_copy(
+                    src_ref=y_buf.at[0, 0, index],
+                    dst_ref=out_ref.at[:, :, columns_of(slot, index)],
+                    send_sem=y_send.at[0, 0, index],
+                    recv_sem=y_recv.at[slot, index],
+                    device_id=(lax.rem(me + 1, positions), tok),
+                    device_id_type=MESH,
+                ).wait_recv()
 
     @pl.when(is_worker)
     def _():
@@ -342,7 +344,8 @@
         for step in range(1, positions):
             lat_copy(1, step).wait_send()
         for target in range(layers):
-            y_copy(1, target).wait_send()
+            for index in range(subs):
+                y_copy(1, target, index).wait_send()
 
 
 def body(inputs, enc_weight, enc_bias, dec_weight, dec_bias):
@@ -352,7 +355,9 @@
     groups = positions // layers
     tok_count = inputs.shape[1]
     width = features // positions
-    chunks = layers + 1
+    sub = min(128, width)
+    subs = width // sub
+    chunks = subs + 1
     vmem = pl.BlockSpec(memory_space=pltpu.VMEM)
     hbm = pl.BlockSpec(memory_space=pltpu.HBM)
     dma = pltpu.SemaphoreType.DMA
@@ -364,9 +369,9 @@
         scratch_shapes=[
             pltpu.VMEM((tok_count, enc_rows * toks), jnp.bfloat16),
             pltpu.VMEM((enc_rows * toks, latent_count), jnp.bfloat16),
-            pltpu.VMEM((pairs, dec_rows * toks, width), jnp.bfloat16),
+            pltpu.VMEM((subs, pairs, dec_rows * toks, sub), jnp.bfloat16),
             pltpu.VMEM((2, positions, tok_count, latent_count), jnp.bfloat16),
-            pltpu.VMEM((2, layers, groups, tok_count, width), jnp.bfloat16),
+            pltpu.VMEM((2, layers, subs, groups, tok_count, sub), jnp.bfloat16),
             dma((chunks,)),
             dma((chunks, toks)),
             dma((chunks, toks)),
@@ -376,8 +381,8 @@
             dma((1,)),
             dma((2, positions)),
             dma((2, positions)),
-            dma((2, layers)),
-            dma((layers,)),
+            dma((2, layers, subs)),
+            dma((layers, subs)),
         ],
         compiler_params=pltpu.CompilerParams(
             collective_id=0, has_side_effects=True, vmem_limit_bytes=58 * 1024 * 1024

time: 155 us -> 136 us (0.88)
  Pallas kernels: 153 us -> 133 us
    pallas_call x1, Pallas kernels: 153 us -> 133 us  [body(): pl.pallas_call(functools.partial(kernel, positions, toks, layers), out_sh...]
where the time goes in v4:
time: 136 us
  Pallas kernels  133 us (98%)
  local copies, waits for them, and re-layouts  2.3 us (2%)
    pallas_call x1, Pallas kernels, body(): pl.pallas_call(functools.partial(kernel, positions, toks, layers), out_sh...  133 us

profile of v4, /device:TPU:0, one launch (start us, length us, event | category | flops | bytes accessed | tf_op | source)
XLA Modules:
  0.0 135.6 jit_solution(1967513972214724449)
XLA Ops:
  0.0 133.3 %shard_map.55 = bf16[1,256,2048]{2,1,0:T(8,128)(2,1)} custom-call(bf16[256,2048]{1,0:T(8,128)(2,1)} %bitcast.3, bf16[4,256,1024]{2,1,0:T(8,128)(2,1)} %enc_ref.1, f32[4,1024]{1,0:T(4,128)} %enc_bias_ref.1, bf16[10,128,2048]{2,1,0:T(8,128)(2,1)} %dec_ref.1, f32[4,2048]{1,0:T(4,128)} %dec_bias_ref.1), custom_call_target="tpu_custom_call" | custom-call | flops 3221225472 | bytes 8388608 | tf_op jit(solution)/shard_map/pallas_call | solution.py:364
  133.3 2.3 %copy.7 = bf16[1,1,256,2048]{3,2,1,0:T(8,128)(2,1)} copy(bf16[1,1,256,2048]{3,2,1,0:T(8,128)(2,1)} %bitcast.2) | data formatting | bytes 2097152

commit v5 on v4

--- a/solution.py
+++ b/solution.py
@@ -273,13 +273,15 @@
         for target in range(layers):
             decode(part_of, target, chunk - 1)
 
+    def helper_compute(chunk):
+        @pl.when(is_helper)
+        def _():
+            compute(chunk, 1)
+
     def compute_both(chunk):
         wait_sibling(chunk)
         compute(chunk, 0)
-
-        @pl.when(is_helper)
-        def _():
-            compute(chunk, 1)
+        helper_compute(chunk)
 
     @pl.when(is_end)
     def _():
@@ -304,9 +306,13 @@
                 start_own(later)
             begun = max(begun, ahead)
             forward(chunk)
+            if chunk == 0:
+                wait_sibling(0)
+                compute(0, 0)
             if chunk == 1:
-                compute_both(0)
-        for chunk in range(0 if chunks <= 1 else 1, chunks):
+                helper_compute(0)
+
+        for chunk in range(1, chunks):
             compute_both(chunk)
 
         for target in range(layers):

time: 136 us -> 129 us (0.949)
  Pallas kernels: 133 us -> 126 us
    pallas_call x1, Pallas kernels: 133 us -> 126 us  [body(): pl.pallas_call(functools.partial(kernel, positions, toks, layers), out_sh...]
where the time goes in v5:
time: 129 us; the launch traced here: 128 us
  Pallas kernels  126 us (98%)
  local copies, waits for them, and re-layouts  2.3 us (2%)
    pallas_call x1, Pallas kernels, body(): pl.pallas_call(functools.partial(kernel, positions, toks, layers), out_sh...  126 us

profile of v5, /device:TPU:0, one launch (start us, length us, event | category | flops | bytes accessed | tf_op | source)
XLA Modules:
  0.0 128.0 jit_solution(6563886341638579514)
XLA Ops:
  0.0 125.7 %shard_map.55 = bf16[1,256,2048]{2,1,0:T(8,128)(2,1)} custom-call(bf16[256,2048]{1,0:T(8,128)(2,1)} %bitcast.3, bf16[4,256,1024]{2,1,0:T(8,128)(2,1)} %enc_ref.1, f32[4,1024]{1,0:T(4,128)} %enc_bias_ref.1, bf16[10,128,2048]{2,1,0:T(8,128)(2,1)} %dec_ref.1, f32[4,2048]{1,0:T(4,128)} %dec_bias_ref.1), custom_call_target="tpu_custom_call" | custom-call | flops 3221225472 | bytes 8388608 | tf_op jit(solution)/shard_map/pallas_call | solution.py:370
  125.7 2.3 %copy.7 = bf16[1,1,256,2048]{3,2,1,0:T(8,128)(2,1)} copy(bf16[1,1,256,2048]{3,2,1,0:T(8,128)(2,1)} %bitcast.2) | data formatting | bytes 2097152
